TPU v7x, 32 devices: a whole 2x2x4 slice. The times are simulated.
32 devices in a mesh: dp: 4 (over z), tm: 4 (over y, x), rows: 2 (over core).
Axes of the slice: x: 2, y: 2, z: 4, core: 2. Of those that a mesh axis runs over, the one named last changes fastest.
Arguments:
- queries: bfloat16 [4, 4, 1, 1, 384, 1536], P('dp', 'tm', None, None, None, 'rows'), may hold values from -44 to 44
- keys_values: bfloat16 [4, 4, 1, 1, 384, 2, 1536], P('dp', 'tm', None, None, None, None, 'rows'), may hold values from -5 to 5
- window_offsets: int32 [4, 4, 1, 1, 3], P('dp', 'tm'), may hold values from 0 to 26, as said below
- out_weight: bfloat16 [1536, 1536], P(('rows', 'dp')), may hold values from -0.15625 to 0.15625
- gate: float32 [4, 1536], P('dp'), may hold values from 3 to 30
Outputs:
- mixed: bfloat16 [4, 4, 1, 1, 384, 1536], P('dp', 'tm', None, None, 'rows')
Inputs may be any that keep to these rules, and one draw needn't show every extreme that they name: `window_offsets`: entry 0 of every row is 13; the other 2 entries are distinct offsets other than 13, which may point outside the grid.
All inputs are finite; a program needn't handle non-finite values.
Results may differ from a plain program's by a relative error of at most 0.015.
Values may be sent and summed in bfloat16 or wider, within the bound.
A program may use at most 64 MiB of HBM per device.

v0:
```python
import jax
import jax.numpy as jnp
from jax import lax
from jax.sharding import PartitionSpec as P

HD = 128
DOUT = 1536


def with_halo(block, sides, width):
    for axis, dim in sides:
        count = lax.axis_size(axis)
        forward = [(i, i + 1) for i in range(count - 1)]
        backward = [(target, source) for source, target in forward]
        low = lax.ppermute(
            lax.slice_in_dim(block, block.shape[dim] - width, None, axis=dim), axis, forward
        )
        high = lax.ppermute(lax.slice_in_dim(block, 0, width, axis=dim), axis, backward)
        block = jnp.concatenate([low, block, high], axis=dim)
    return block


def local(queries, keys_values, window_offsets, out_weight, gate):
    nht = queries.shape[2]
    wt = queries.shape[3]
    tl = queries.shape[4]
    local_width = queries.shape[5]
    local_heads = local_width // HD
    tiles = nht * wt
    keep = window_offsets.shape[4]
    scale = float(HD) ** (-0.5)
    extended = with_halo(keys_values, (("tm", 1),), 1)
    ext_flat = extended[0].reshape(3 * tiles, tl, 2, local_width)
    offsets = window_offsets[0, 0]
    all_time = lax.axis_size("tm")
    time_now = lax.axis_index("tm")
    row_pos = jnp.arange(nht, dtype=jnp.int32)[:, None, None]
    col_pos = jnp.arange(wt, dtype=jnp.int32)[None, :, None]
    first = offsets // 9
    near_t = time_now + first - 1
    near_h = row_pos + offsets // 3 % 3 - 1
    near_w = col_pos + offsets % 3 - 1
    inside = (
        (near_t >= 0)
        & (near_t < all_time)
        & (near_h >= 0)
        & (near_h < nht)
        & (near_w >= 0)
        & (near_w < wt)
    )
    index = first * tiles + jnp.clip(near_h, 0, nht - 1) * wt + jnp.clip(near_w, 0, wt - 1)
    index = index.reshape(tiles, keep)
    inside = inside.reshape(tiles, keep)
    q_flat = queries[0, 0].reshape(tiles, tl, local_heads, HD)

    def per_tile(items):
        query_tile, index_row, live_row = items
        key_tiles = jnp.take(ext_flat, index_row, axis=0)
        keys = key_tiles[:, :, 0, :].reshape(keep * tl, local_heads, HD)
        values = key_tiles[:, :, 1, :].reshape(keep * tl, local_heads, HD)
        scores = (
            jnp.einsum("qnd,knd->nqk", query_tile, keys, preferred_element_type=jnp.float32) * scale
        )
        mask = jnp.repeat(live_row, tl)[None, None, :]
        top = jnp.max(jnp.where(mask, scores, -jnp.inf), axis=2, keepdims=True)
        prob = jnp.where(mask, jnp.exp(scores - top), 0.0)
        total = jnp.sum(prob, axis=2, keepdims=True)
        weights = (prob / total).astype(jnp.bfloat16)
        acc = jnp.einsum("nqk,knd->qnd", weights, values, preferred_element_type=jnp.float32)
        return acc.astype(jnp.bfloat16).reshape(tl, local_width)

    attended = lax.map(per_tile, (q_flat, index, inside))
    bands = lax.axis_size("rows")
    band = tl // bands
    reordered = (
        attended.reshape(tiles, bands, band, local_width)
        .transpose(1, 0, 2, 3)
        .reshape(tiles * tl, local_width)
    )
    head_rows = lax.all_gather(out_weight, "dp", axis=0, tiled=True)
    projection = lax.psum_scatter(
        jnp.dot(reordered, head_rows, preferred_element_type=jnp.float32),
        "rows",
        scatter_dimension=0,
        tiled=True,
    )
    mixed = (gate[0][None, :] * projection).astype(jnp.bfloat16)
    return mixed.reshape(1, 1, nht, wt, band, DOUT)


def solution(mesh):
    placed = (
        P("dp", "tm", None, None, None, "rows"),
        P("dp", "tm", None, None, None, None, "rows"),
        P("dp", "tm", None, None, None),
        P(("rows", "dp"), None),
        P("dp", None),
    )
    return jax.shard_map(
        local,
        mesh=mesh,
        in_specs=placed,
        out_specs=P("dp", "tm", None, None, "rows", None),
        check_vma=False,
    )
```

profile of v0, /device:TPU:11, one launch (start us, length us, event | category | flops | bytes accessed | tf_op | source)
XLA Modules:
  0.0 154.5 jit_solution(8666616512665643484)
XLA Ops:
  6.5 0.0 all-gather.2.cloned.1.call-start
  6.5 3.1 %collective-permute-start = (bf16[1,1,1,1,384,2,768]{6,5,4,3,2,1,0:T(2,128)(2,1)}, bf16[1,1,1,1,384,2,768]{6,5,4,3,2,1,0:T(2,128)(2,1)S(1)}, u32[]{:S(2)}, u32[]{:S(2)}) collective-permute-start(bf16[1,1,1,1,384,2,768]{6,5,4,3,2,1,0:T(2,128)(2,1)} %param.6), channel_id=1, source_target_pairs={{0,2},{2,4},{4,6},{1,3},{3,5},{5,7},{8,10},{10,12},{12,14},{9,11},... | collective-permute-start | bytes 3538952 | tf_op jit(solution)/shard_map/ppermute | solution.py:15
  9.7 2.2 %collective-permute-start.1 = (bf16[1,1,1,1,384,2,768]{6,5,4,3,2,1,0:T(2,128)(2,1)}, bf16[1,1,1,1,384,2,768]{6,5,4,3,2,1,0:T(2,128)(2,1)S(1)}, u32[]{:S(2)}, u32[]{:S(2)}) collective-permute-start(bf16[1,1,1,1,384,2,768]{6,5,4,3,2,1,0:T(2,128)(2,1)} %param.6), channel_id=1, source_target_pairs={{2,0},{4,2},{6,4},{3,1},{5,3},{7,5},{10,8},{12,10},{14,12},{11,9},... | collective-permute-start | bytes 3538952 | tf_op jit(solution)/shard_map/ppermute | solution.py:18
  11.9 0.0 all-gather.2.cloned.1.call-update
  11.9 0.0 reduce-scatter.2.cloned.1.call-start
  12.0 2.1 %copy.9 = bf16[1,1,1,1,384,768]{4,5,3,2,1,0:T(8,128)(2,1)} copy(bf16[1,1,1,1,384,768]{5,4,3,2,1,0:T(8,128)(2,1)} %param.5) | data formatting | bytes 1179648 | tf_op args[0]
  14.1 0.7 compare_and_fusion
  14.8 0.1 broadcast_in_dim.52
  14.9 0.7 fusion.34
  15.6 0.7 compare_and_fusion.1
  16.3 19.3 %collective-permute-done = bf16[1,1,1,1,384,2,768]{6,5,4,3,2,1,0:T(2,128)(2,1)S(1)} collective-permute-done((bf16[1,1,1,1,384,2,768]{6,5,4,3,2,1,0:T(2,128)(2,1)}, bf16[1,1,1,1,384,2,768]{6,5,4,3,2,1,0:T(2,128)(2,1)S(1)}, u32[]{:S(2)}, u32[]{:S(2)}) %collective-permute-start) | collective-permute-done | bytes 1179680 | tf_op jit(solution)/shard_map/ppermute | solution.py:15
  35.6 26.2 %collective-permute-done.1 = bf16[1,1,1,1,384,2,768]{6,5,4,3,2,1,0:T(2,128)(2,1)S(1)} collective-permute-done((bf16[1,1,1,1,384,2,768]{6,5,4,3,2,1,0:T(2,128)(2,1)}, bf16[1,1,1,1,384,2,768]{6,5,4,3,2,1,0:T(2,128)(2,1)S(1)}, u32[]{:S(2)}, u32[]{:S(2)}) %collective-permute-start.1) | collective-permute-done | bytes 1179680 | tf_op jit(solution)/shard_map/ppermute | solution.py:18
  61.8 8.5 %maximum_bitcast_fusion = bf16[3,384,2,768]{3,2,1,0:T(2,128)(2,1)} fusion(bf16[1,1,1,1,384,2,768]{6,5,4,3,2,1,0:T(2,128)(2,1)S(1)} %collective-permute-done.1, bf16[1,1,1,1,384,2,768]{6,5,4,3,2,1,0:T(2,128)(2,1)} %param.6, bf16[1,1,1,1,384,2,768]{6,5,4,3,2,1,0:T(2,128)(2,1)S(1)} %collective-permute-done), kind=kLoop, calls=%fused_computation.16 | loop fusion | flops 3538944 | bytes 7077888 | tf_op jit(solution)/shard_map/reshape;squeeze | solution.py:33
  70.3 10.0 %gather_fusion = bf16[3,384,2,768]{3,2,1,0:T(2,128)(2,1)S(1)} fusion(bf16[3,384,2,768]{3,2,1,0:T(2,128)(2,1)} %maximum_bitcast_fusion, s32[1024]{0:T(1024)S(1)} %pad_clamp_fusion), kind=kCustom, calls=%fused_computation | custom fusion | bytes 7077900 | tf_op jit(solution)/shard_map/while/body/eval_jaxpr/jit(_take)/gather | solution.py:58
  80.3 3.1 %broadcast_select_fusion = bf16[3,384,2,768]{3,2,1,0:T(2,128)(2,1)S(1)} fusion(bf16[3,384,2,768]{3,2,1,0:T(2,128)(2,1)S(1)} %gather_fusion, pred[3]{0:T(512)(128)(4,1)S(1)} %compare_and_fusion.1), kind=kLoop, calls=%fused_computation.9 | loop fusion | flops 1769472 | bytes 7077891 | tf_op jit(solution)/shard_map/while/body/eval_jaxpr/jit(_take)/select_n | solution.py:58
  83.4 22.2 %slice_reduce_fusion.1 = (bf16[3,384,768]{2,1,0:T(8,128)(2,1)}, bf16[3,384,768]{2,1,0:T(8,128)(2,1)}) fusion(bf16[3,384,2,768]{3,2,1,0:T(2,128)(2,1)S(1)} %broadcast_select_fusion), kind=kLoop, calls=%fused_computation.15 | loop fusion | bytes 7077888 | tf_op jit(solution)/shard_map/while/body/eval_jaxpr/slice | solution.py:60
  105.6 3.6 %squeeze.21 = bf16[1152,6,128]{2,1,0:T(8,128)(2,1)S(1)} reshape(bf16[3,384,768]{2,1,0:T(8,128)(2,1)} %get-tuple-element.16) | data formatting | bytes 3538944 | tf_op jit(solution)/shard_map/while/body/eval_jaxpr/reshape;while/body/eval_jaxpr/squeeze | solution.py:59
  109.2 4.9 %squeeze.20 = bf16[1152,6,128]{2,1,0:T(8,128)(2,1)} reshape(bf16[3,384,768]{2,1,0:T(8,128)(2,1)} %get-tuple-element.15) | data formatting | bytes 3538944 | tf_op jit(solution)/shard_map/while/body/eval_jaxpr/reshape;while/body/eval_jaxpr/squeeze | solution.py:60
  114.1 2.6 %fusion.12 = f32[6,1152,384]{2,1,0:T(8,128)S(1)} fusion(bf16[384,6,128]{0,2,1:T(8,128)(2,1)} %bitcast.91, bf16[1152,6,128]{2,1,0:T(8,128)(2,1)S(1)} %squeeze.21), kind=kOutput, calls=%fused_computation.18 | convolution fusion | flops 679477248 | bytes 12976128 | tf_op jit(solution)/shard_map/while/body/eval_jaxpr/qnd,knd->nqk/dot_general | solution.py:62
  116.7 0.0 copy-start
  116.7 7.3 %bitcast_reduce_fusion = (f32[6,384]{1,0:T(8,128)S(1)}, f32[6,1152,384]{2,1,0:T(8,128)}) fusion(f32[6,1152,384]{2,1,0:T(8,128)S(1)} %fusion.12, pred[1152]{0:T(1024)(128)(4,1)S(1)} %broadcast_in_dim.53), kind=kOutput, calls=%fused_computation.3 | output fusion | flops 15926399 | bytes 21244032 | tf_op jit(solution)/shard_map/while/body/eval_jaxpr/sub | solution.py:66
  124.0 0.0 copy-done
  124.0 5.5 %fusion.14 = bf16[6,128,384]{2,1,0:T(8,128)(2,1)S(1)} fusion(f32[6,1152,384]{2,1,0:T(8,128)} %get-tuple-element.29, f32[6,384]{1,0:T(8,128)S(1)} %get-tuple-element.28, bf16[1152,6,128]{2,1,0:T(8,128)(2,1)S(1)} %copy-done), kind=kOutput, calls=%fused_computation.20 | convolution fusion | flops 685080576 | bytes 12985344 | tf_op jit(solution)/shard_map/while/body/eval_jaxpr/nqk,knd->qnd/dot_general | solution.py:69
  129.5 0.0 all-gather.2.cloned.1.call-done
  129.5 0.0 copy-start.1
  129.5 4.2 %fusion.39 = f32[384,1536]{1,0:T(8,128)} fusion(bf16[384,768]{0,1:T(8,128)(2,1)S(1)} %bitcast.92, bf16[768,1536]{1,0:T(8,128)(2,1)} %all-gather.2.cloned.1.call-done), kind=kOutput, calls=%fused_computation.57 | convolution fusion | flops 905969664 | bytes 5308416 | tf_op jit(solution)/shard_map/dot_general | solution.py:82
  133.7 0.0 reduce-scatter.2.cloned.1.call-update
  133.7 0.0 copy-done.1
  133.8 11.7 %reduce-scatter.2.cloned.1.call-done = f32[192,1536]{1,0:T(8,128)} async-done(((f32[384,1536]{1,0:T(8,128)}), f32[192,1536]{1,0:T(8,128)}) %reduce-scatter.2.cloned.1.call-update) | async-done | bytes 1179664 | tf_op jit(solution)/shard_map/reduce_scatter | solution.py:81
  145.5 2.2 %fusion.19 = bf16[1,1,1,1,192,1536]{5,4,3,2,1,0:T(8,128)(2,1)} fusion(f32[192,1536]{1,0:T(8,128)} %reduce-scatter.2.cloned.1.call-done, f32[1536]{0:T(1024)S(1)} %reduce.1), kind=kLoop, calls=%fused_computation.22 | loop fusion | flops 589824 | bytes 1775616 | tf_op jit(solution)/shard_map/reshape | solution.py:88
  (3 shorter events, 0.1 us)
Async XLA Ops:
  6.5 122.9 %all-gather.2.cloned.1.call-start = ((), (), s32[]{:S(2)}) async-start(), calls=%async_computation.1 | async-start | bytes 2949120 | tf_op jit(solution)/shard_map/all_gather | solution.py:80
  6.5 29.0 %collective-permute-start = (bf16[1,1,1,1,384,2,768]{6,5,4,3,2,1,0:T(2,128)(2,1)}, bf16[1,1,1,1,384,2,768]{6,5,4,3,2,1,0:T(2,128)(2,1)S(1)}, u32[]{:S(2)}, u32[]{:S(2)}) collective-permute-start(bf16[1,1,1,1,384,2,768]{6,5,4,3,2,1,0:T(2,128)(2,1)} %param.6), channel_id=1, source_target_pairs={{0,2},{2,4},{4,6},{1,3},{3,5},{5,7},{8,10},{10,12},{12,14},{9,11},... | collective-permute-start | bytes 3538952 | tf_op jit(solution)/shard_map/ppermute | solution.py:15
  9.7 52.2 %collective-permute-start.1 = (bf16[1,1,1,1,384,2,768]{6,5,4,3,2,1,0:T(2,128)(2,1)}, bf16[1,1,1,1,384,2,768]{6,5,4,3,2,1,0:T(2,128)(2,1)S(1)}, u32[]{:S(2)}, u32[]{:S(2)}) collective-permute-start(bf16[1,1,1,1,384,2,768]{6,5,4,3,2,1,0:T(2,128)(2,1)} %param.6), channel_id=1, source_target_pairs={{2,0},{4,2},{6,4},{3,1},{5,3},{7,5},{10,8},{12,10},{14,12},{11,9},... | collective-permute-start | bytes 3538952 | tf_op jit(solution)/shard_map/ppermute | solution.py:18
  11.9 133.5 %reduce-scatter.2.cloned.1.call-start = ((), (), s32[]{:S(2)}) async-start(), calls=%async_computation.2 | async-start | bytes 3538944 | tf_op jit(solution)/shard_map/reduce_scatter | solution.py:81
  116.7 7.3 %copy-start = (bf16[1152,6,128]{2,1,0:T(8,128)(2,1)S(1)}, bf16[1152,6,128]{2,1,0:T(8,128)(2,1)}, u32[]{:S(2)}) copy-start(bf16[1152,6,128]{2,1,0:T(8,128)(2,1)} %squeeze.20) | copy-start | bytes 5308420
  129.5 4.2 %copy-start.1 = (f32[1,1536]{1,0:T(1,128)S(1)}, f32[1,1536]{1,0:T(1,128)}, u32[]{:S(2)}) copy-start(f32[1,1536]{1,0:T(1,128)} %param.9) | copy-start | bytes 18436
Sparse Core Ops, SparseCore 0:
  12.0 50.3 all-gather.1
  133.8 11.5 reduce-scatter.1
where the time goes:
time: 156 us; the launch traced here: 154 us
  waiting for transfers between devices  57.3 us (37%)
  local copies, waits for them, and re-layouts  42.9 us (28%)
  other arithmetic  23.1 us (15%)
  between operations  13.5 us (9%)
  matrix products  12.2 us (8%)
  starting transfers between devices  5.39 us (3%)
    ppermute x1, waiting for transfers between devices, with_halo(): lax.ppermute(lax.slice_in_dim(block, 0, width, axis=dim), axis, backward)  26.2 us
    slice x1, local copies, waits for them, and re-layouts, per_tile(): values = key_tiles[:, :, 1, :].reshape(keep * tl, local_heads, HD)  22.2 us
    ppermute x1, waiting for transfers between devices, with_halo(): lax.ppermute(lax.slice_in_dim(block, block.shape[dim] - width, None, axis...  19.3 us
    reduce_scatter x1, waiting for transfers between devices, local(): lax.psum_scatter(jnp.dot(reordered, head_rows, preferred_element_type=jnp...  11.7 us
    gather x1, local copies, waits for them, and re-layouts, per_tile(): key_tiles = jnp.take(ext_flat, index_row, axis=0)  9.99 us
    another operation x1, other arithmetic, local(): ext_flat = extended[0].reshape(3 * tiles, tl, 2, local_width)  8.47 us
    sub x1, other arithmetic, per_tile(): prob = jnp.where(mask, jnp.exp(scores - top), 0.0)  7.27 us
    dot_general x1, matrix products, per_tile(): jnp.einsum('nqk,knd->qnd', weights, values, preferred_element_type=jnp.fl...  5.47 us
  transfers between devices with their start and end apart: 4, of which 3 were waited for; matrix products, arithmetic and copies ran while one was open for 47% of the time, Pallas kernels for 0%

commit v1 on v0

v1 whole, which is shorter than its diff:
```python
import functools
import math

import jax
import jax.numpy as jnp
from jax import lax
from jax.experimental import pallas as pl
from jax.experimental.pallas import tpu as pltpu
from jax.sharding import PartitionSpec as P

HD = 128
MESH = pl.DeviceIdType.MESH
PARTS = 2
PLAN = {1: 1, 2: 1, 4: 1, 5: 1}


def kernel(
    ndp,
    ntm,
    heads,
    off_ref,
    q_ref,
    kv_ref,
    w_ref,
    gate_ref,
    out_ref,
    a_buf,
    b_buf,
    wbuf,
    att,
    att_send,
    a_send,
    a_recv,
    b_send,
    b_recv,
    z_send,
    z_recv,
    c_send,
    c_recv,
    own_send,
    own_recv,
    own_local,
    att_sem,
):
    i = lax.axis_index("dp")
    t = lax.axis_index("tm")
    r = lax.axis_index("rows")
    other = 1 - r
    relay = ntm == 4
    odd = t % 2
    partner = t + 1 - 2 * odd
    beyond = t - 1 + 2 * odd
    has_b = jnp.logical_and(beyond >= 0, beyond < ntm)
    if relay:
        b_target = (t + 2) % 4
        b_sends = jnp.logical_not(has_b)
        greets_b = t >= 0
    else:
        b_target = jnp.clip(beyond, 0, ntm - 1)
        b_sends = has_b
        greets_b = has_b
    has_left = i > 0
    has_right = i < ndp - 1
    left = jnp.maximum(i - 1, 0)
    right = jnp.minimum(i + 1, ndp - 1)
    band = out_ref.shape[0]
    rows = w_ref.shape[0]
    piece = rows // PARTS
    events = PARTS * (ndp - 1)

    barrier = pltpu.get_barrier_semaphore()

    def greet(device):
        pl.semaphore_signal(barrier, inc=1, device_id=device, device_id_type=MESH)

    greet({"rows": other})
    greet({"tm": partner})

    @pl.when(greets_b)
    def _():
        greet({"tm": b_target})

    @pl.when(has_left)
    def _():
        greet({"dp": left})

    @pl.when(has_right)
    def _():
        greet({"dp": right})

    peers = 2
    for present in (greets_b, has_left, has_right):
        peers = peers + jnp.where(present, 1, 0)
    pl.semaphore_wait(barrier, peers)

    def remote(src, dst, send, recv, device):
        return pltpu.make_async_remote_copy(
            src_ref=src, dst_ref=dst, send_sem=send, recv_sem=recv, device_id=device, device_id_type=MESH
        )

    def a_copy(h):
        return remote(kv_ref.at[h], a_buf.at[h], a_send.at[h], a_recv.at[h], {"tm": partner})

    def b_copy(h):
        src = a_buf if relay else kv_ref
        return remote(src.at[h], b_buf.at[h], b_send.at[h], b_recv.at[h], {"tm": b_target})

    def place(half, shard, part):
        start = pl.multiple_of((half * ndp + shard) * rows + part * piece, 16)
        return wbuf.at[pl.ds(start, piece)]

    def own_piece(part):
        return w_ref.at[pl.ds(part * piece, piece)]

    def z_copy(src, shard, part, side, event):
        target = right if side == 0 else left
        return remote(
            src, place(r, shard, part), z_send.at[side, event], z_recv.at[side, event], {"dp": target}
        )

    def c_copy(shard, part, side, event):
        spot = place(r, shard, part)
        return remote(spot, spot, c_send.at[side, event], c_recv.at[side, event], {"rows": other})

    def shard_of(step, side):
        return i - 1 - step if side == 0 else i + 1 + step

    def valid(step, side):
        shard = shard_of(step, side)
        return shard >= 0 if side == 0 else shard < ndp

    sends_on = (has_right, has_left)

    for h in range(min(2, heads)):
        a_copy(h).start()
    for part in range(PARTS):
        for side in (0, 1):
            @pl.when(sends_on[side])
            def _():
                z_copy(own_piece(part), i, part, side, part).start()
    own_spot = wbuf.at[pl.ds(pl.multiple_of((r * ndp + i) * rows, 16), rows)]
    own_copy = pltpu.make_async_copy(w_ref, own_spot, own_local)
    own_copy.start()
    own_across = remote(w_ref, own_spot, own_send, own_recv, {"rows": other})
    own_across.start()
    if not relay:
        @pl.when(b_sends)
        def _():
            for h in range(heads):
                b_copy(h).start()

    @pl.when(jnp.logical_not(has_b))
    def _():
        b_buf[...] = jnp.zeros_like(b_buf)

    def weight_event(event):
        step, part = event // PARTS, event % PARTS
        for side in (0, 1):
            @pl.when(valid(step, side))
            def _():
                shard = shard_of(step, side)
                spot = place(r, shard, part)
                z_copy(spot, shard, part, side, event).wait_recv()

                @pl.when(sends_on[side])
                def _():
                    z_copy(spot, shard, part, side, event + PARTS).start()

                c_copy(shard, part, side, event).start()

    def is_live(code):
        hit = off_ref[0] == code
        for k in range(1, off_ref.shape[0]):
            hit = jnp.logical_or(hit, off_ref[k] == code)
        return hit

    low = is_live(4)
    high = is_live(22)
    a_live = jnp.logical_or(jnp.logical_and(low, odd == 1), jnp.logical_and(high, odd == 0))
    b_live = jnp.logical_or(jnp.logical_and(low, odd == 0), jnp.logical_and(high, odd == 1))
    b_live = jnp.logical_and(b_live, has_b)
    dead = jnp.float32(-jnp.inf)
    a_bias = jnp.where(a_live, jnp.float32(0), dead)
    b_bias = jnp.where(b_live, jnp.float32(0), dead)
    factor = HD**-0.5 * math.log2(math.e)

    def score(q, keys):
        return lax.dot_general(
            q, keys, (((1,), (1,)), ((), ())), preferred_element_type=jnp.float32
        )

    def attend(h, which):
        q = q_ref[pl.ds(pl.multiple_of(which * band, 16), band), h * HD : (h + 1) * HD]
        parts = (
            score(q, kv_ref[h, 0]),
            score(q, a_buf[h, 0]) + a_bias,
            score(q, b_buf[h, 0]) + b_bias,
        )
        top = functools.reduce(
            jnp.maximum, [jnp.max(s, axis=1, keepdims=True) for s in parts]
        )
        total = 0.0
        acc = 0.0
        for s, held in zip(parts, (kv_ref, a_buf, b_buf)):
            p = jnp.exp2((s - top) * factor)
            total = total + jnp.sum(p, axis=1, keepdims=True)
            acc = acc + jnp.dot(
                p.astype(jnp.bfloat16), held[h, 1], preferred_element_type=jnp.float32
            )
        return (acc / total).astype(jnp.bfloat16)

    done = 0
    for h in range(heads + 1):
        if h < heads:
            a_copy(h).wait_recv()
            if h + 2 < heads:
                a_copy(h + 2).start()
            if relay:
                @pl.when(b_sends)
                def _():
                    b_copy(h).start()
        if ndp == 4:
            for _ in range(PLAN.get(h, 0)):
                weight_event(done)
                done += 1
        if h > 0:
            g = h - 1

            @pl.when(has_b)
            def _():
                b_copy(g).wait_recv()

            columns = pl.ds(g * HD, HD)
            att_send[:, columns] = attend(g, other)
            att[r, :, columns] = attend(g, r)

    across = remote(att_send, att.at[r], att_sem.at[0], att_sem.at[1], {"rows": other})
    across.start()

    def later(event, carry):
        weight_event(event)
        return carry

    lax.fori_loop(done, events, later, 0)

    own_copy.wait()
    own_across.wait_recv()
    across.wait_recv()

    def settle(event, carry):
        step, part = event // PARTS, event % PARTS
        for side in (0, 1):
            @pl.when(valid(step, side))
            def _():
                c_copy(shard_of(step, side), part, side, event).wait_recv()
        return carry

    lax.fori_loop(0, events, settle, 0)

    half = wbuf.shape[0] // 2
    width = out_ref.shape[1]
    tile = 512 if width % 512 == 0 else width
    for start in range(0, width, tile):
        columns = pl.ds(start, tile)
        product = jnp.dot(att[0], wbuf[:half, columns], preferred_element_type=jnp.float32)
        product += jnp.dot(att[1], wbuf[half:, columns], preferred_element_type=jnp.float32)
        out_ref[:, columns] = (gate_ref[:, columns] * product).astype(out_ref.dtype)

    for h in range(heads):
        a_copy(h).wait_send()

    @pl.when(b_sends)
    def _():
        for h in range(heads):
            b_copy(h).wait_send()

    own_across.wait_send()
    across.wait_send()

    def sent_own(part, carry):
        for side in (0, 1):
            @pl.when(sends_on[side])
            def _():
                z_copy(own_piece(part), i, part, side, part).wait_send()
        return carry

    for part in range(PARTS):
        sent_own(part, 0)

    def sent(event, carry):
        step, part = event // PARTS, event % PARTS
        for side in (0, 1):
            @pl.when(valid(step, side))
            def _():
                shard = shard_of(step, side)
                c_copy(shard, part, side, event).wait_send()

                @pl.when(sends_on[side])
                def _():
                    z_copy(place(r, shard, part), shard, part, side, event + PARTS).wait_send()
        return carry

    lax.fori_loop(0, events, sent, 0)


def local(queries, keys_values, window_offsets, out_weight, gate):
    tl, width = queries.shape[4], queries.shape[5]
    heads = width // HD
    ndp, ntm, bands = lax.axis_size("dp"), lax.axis_size("tm"), lax.axis_size("rows")
    assert queries.shape[2] == queries.shape[3] == 1 and bands == 2 and ntm % 2 == 0
    band = tl // bands
    rows, dout = out_weight.shape
    events = PARTS * (ndp - 1)
    kv = keys_values.reshape(tl, 2, heads, HD).transpose(2, 1, 0, 3)
    bf16 = jnp.bfloat16
    vmem = pl.BlockSpec(memory_space=pltpu.VMEM)
    dma = pltpu.SemaphoreType.DMA
    mixed = pl.pallas_call(
        functools.partial(kernel, ndp, ntm, heads),
        out_shape=jax.ShapeDtypeStruct((band, dout), bf16),
        in_specs=[pl.BlockSpec(memory_space=pltpu.SMEM), vmem, vmem, vmem, vmem],
        out_specs=vmem,
        scratch_shapes=[
            pltpu.VMEM((heads, 2, tl, HD), bf16),
            pltpu.VMEM((heads, 2, tl, HD), bf16),
            pltpu.VMEM((2 * ndp * rows, dout), bf16),
            pltpu.VMEM((2, band, width), bf16),
            pltpu.VMEM((band, width), bf16),
            dma((heads,)),
            dma((heads,)),
            dma((heads,)),
            dma((heads,)),
            dma((2, events + PARTS)),
            dma((2, events + PARTS)),
            dma((2, events)),
            dma((2, events)),
            dma,
            dma,
            dma,
            dma((2,)),
        ],
        compiler_params=pltpu.CompilerParams(
            collective_id=0, has_side_effects=True, vmem_limit_bytes=48 * 1024 * 1024
        ),
        cost_estimate=pl.CostEstimate(
            flops=4 * 3 * tl * tl * width + 4 * band * width * dout,
            bytes_accessed=2 * (3 * tl * width + rows * dout + band * dout),
            transcendentals=3 * tl * tl * heads,
        ),
    )(window_offsets.reshape(-1), queries.reshape(tl, width), kv, out_weight, gate)
    return mixed.reshape(1, 1, 1, 1, band, dout)


def solution(mesh):
    placed = (
        P("dp", "tm", None, None, None, "rows"),
        P("dp", "tm", None, None, None, None, "rows"),
        P("dp", "tm", None, None, None),
        P(("rows", "dp"), None),
        P("dp", None),
    )
    return jax.shard_map(
        local,
        mesh=mesh,
        in_specs=placed,
        out_specs=P("dp", "tm", None, None, "rows", None),
        check_vma=False,
    )
```

time: 156 us -> 52.5 us (0.34)
  the two profiles are of different devices: /device:TPU:11 before, /device:TPU:1 now
where the time goes in v1:
time: 52.5 us; the launch traced here: 52.3 us
  Pallas kernels  46.6 us (89%)
  local copies, waits for them, and re-layouts  5.62 us (11%)
    pallas_call x1, Pallas kernels, local(): pl.pallas_call(functools.partial(kernel, ndp, ntm, heads), out_shape=jax....  46.6 us
    unnamed x10, local copies, waits for them, and re-layouts  4.85 us

profile of v1, /device:TPU:1, one launch (start us, length us, event | category | flops | bytes accessed | tf_op | source)
XLA Modules:
  0.0 52.3 jit_solution(10086866329831067965)
XLA Ops:
  0.0 3.6 %copy.6 = bf16[1,1,1,1,384,2,768]{4,6,5,3,2,1,0:T(8,128)(2,1)S(1)} copy(bf16[1,1,1,1,384,2,768]{6,5,4,3,2,1,0:T(2,128)(2,1)} %param.6) | data formatting | bytes 2359296 | tf_op args[1]
  3.6 0.0 copy-start
  3.6 0.0 copy-start.1
  3.6 0.0 copy-start.2
  3.6 0.0 copy-start.3
  3.6 0.8 %copy.7 = bf16[384,2,6,128]{3,0,1,2:T(8,128)(2,1)S(1)} copy(bf16[384,2,6,128]{0,3,2,1:T(8,128)(2,1)S(1)} %bitcast.9) | data formatting | bytes 2359296 | tf_op jit(solution)/shard_map/reshape | solution.py:314
  4.4 0.2 copy-done
  4.7 0.2 copy-done.1
  4.8 0.0 copy-done.2
  4.8 0.0 copy-done.3
  4.8 46.6 %shard_map.55 = bf16[192,1536]{1,0:T(8,128)(2,1)S(1)} custom-call(s32[3]{0:T(128)S(1)} %bitcast.8, bf16[384,768]{1,0:T(8,128)(2,1)S(1)} %bitcast.7, bf16[6,2,384,128]{3,2,1,0:T(8,128)(2,1)S(1)} %bitcast.5, bf16[192,1536]{1,0:T(8,128)(2,1)S(1)} %copy-done.1, f32[1,1536]{1,0:T(1,128)S(1)} %copy-done.2), custom_call_target="tpu_custom_call" | custom-call | flops 2264924160 | bytes 2949120 | tf_op jit(solution)/shard_map/pallas_call | solution.py:318
  51.5 0.8 %copy.9 = bf16[1,1,1,1,192,1536]{5,4,3,2,1,0:T(8,128)(2,1)} copy(bf16[1,1,1,1,192,1536]{5,4,3,2,1,0:T(8,128)(2,1)S(1)} %bitcast.6) | data formatting | bytes 1179648
Async XLA Ops:
  3.6 1.1 %copy-start = (bf16[1,1,1,1,384,768]{5,4,3,2,1,0:T(8,128)(2,1)S(1)}, bf16[1,1,1,1,384,768]{5,4,3,2,1,0:T(8,128)(2,1)}, u32[]{:S(2)}) copy-start(bf16[1,1,1,1,384,768]{5,4,3,2,1,0:T(8,128)(2,1)} %param.5) | copy-start | bytes 1769476
  3.6 1.2 %copy-start.1 = (bf16[192,1536]{1,0:T(8,128)(2,1)S(1)}, bf16[192,1536]{1,0:T(8,128)(2,1)}, u32[]{:S(2)}) copy-start(bf16[192,1536]{1,0:T(8,128)(2,1)} %w_ref.1) | copy-start | bytes 1769476
  3.6 1.2 %copy-start.2 = (f32[1,1536]{1,0:T(1,128)S(1)}, f32[1,1536]{1,0:T(1,128)}, u32[]{:S(2)}) copy-start(f32[1,1536]{1,0:T(1,128)} %gate_ref.1) | copy-start | bytes 18436
  3.6 1.2 %copy-start.3 = (s32[1,1,1,1,3]{4,3,2,1,0:T(1,128)S(1)}, s32[1,1,1,1,3]{4,3,2,1,0:T(1,128)}, u32[]{:S(2)}) copy-start(s32[1,1,1,1,3]{4,3,2,1,0:T(1,128)} %param.7) | copy-start | bytes 40

commit v2 on v1

--- a/solution.py
+++ b/solution.py
@@ -10,8 +10,7 @@
 
 HD = 128
 MESH = pl.DeviceIdType.MESH
-PARTS = 2
-PLAN = {1: 1, 2: 1, 4: 1, 5: 1}
+PLAN = {0: (1, 0), 1: (1, 1), 2: (2, 0), 3: (1, 0), 4: (1, 1), 5: (1, 0), 6: (1, 1)}
 
 
 def kernel(
@@ -20,15 +19,18 @@
     heads,
     off_ref,
     q_ref,
-    kv_ref,
+    kv_in,
     w_ref,
     gate_ref,
     out_ref,
+    kv_ref,
     a_buf,
     b_buf,
     wbuf,
     att,
     att_send,
+    att_cut,
+    total_ref,
     a_send,
     a_recv,
     b_send,
@@ -37,6 +39,10 @@
     z_recv,
     c_send,
     c_recv,
+    y_send,
+    y_recv,
+    d_send,
+    d_recv,
     own_send,
     own_recv,
     own_local,
@@ -65,8 +71,21 @@
     right = jnp.minimum(i + 1, ndp - 1)
     band = out_ref.shape[0]
     rows = w_ref.shape[0]
-    piece = rows // PARTS
-    events = PARTS * (ndp - 1)
+    steps = ndp - 1
+    upper = t // 2
+    if relay and rows % 192 == 0:
+        edge, inner = rows // 6, rows // 3
+        pieces = ((upper * (rows - edge), edge), (edge, inner), (edge + inner, inner))
+        far_piece = ((1 - upper) * (rows - edge), edge)
+        shared = True
+    else:
+        pieces = ((0, rows // 2), (rows // 2, rows // 2))
+        far_piece = pieces[0]
+        shared = False
+    parts = len(pieces)
+
+    def deinterleave(h):
+        kv_ref[h] = jnp.swapaxes(kv_in[:, :, h * HD : (h + 1) * HD], 0, 1)
 
     barrier = pltpu.get_barrier_semaphore()
 
@@ -87,6 +106,13 @@
     @pl.when(has_right)
     def _():
         greet({"dp": right})
+
+    for h in range(min(2, heads)):
+        deinterleave(h)
+
+    @pl.when(jnp.logical_not(has_b))
+    def _():
+        b_buf[...] = jnp.zeros_like(b_buf)
 
     peers = 2
     for present in (greets_b, has_left, has_right):
@@ -105,22 +131,39 @@
         src = a_buf if relay else kv_ref
         return remote(src.at[h], b_buf.at[h], b_send.at[h], b_recv.at[h], {"tm": b_target})
 
-    def place(half, shard, part):
-        start = pl.multiple_of((half * ndp + shard) * rows + part * piece, 16)
-        return wbuf.at[pl.ds(start, piece)]
+    def place(half, shard, spot):
+        start = pl.multiple_of((half * ndp + shard) * rows + spot[0], 16)
+        return wbuf.at[pl.ds(start, spot[1])]
 
     def own_piece(part):
-        return w_ref.at[pl.ds(part * piece, piece)]
-
-    def z_copy(src, shard, part, side, event):
+        first, size = pieces[part]
+        return w_ref.at[pl.ds(pl.multiple_of(first, 16), size)]
+
+    def z_copy(src, shard, part, side, step):
         target = right if side == 0 else left
         return remote(
-            src, place(r, shard, part), z_send.at[side, event], z_recv.at[side, event], {"dp": target}
-        )
-
-    def c_copy(shard, part, side, event):
-        spot = place(r, shard, part)
-        return remote(spot, spot, c_send.at[side, event], c_recv.at[side, event], {"rows": other})
+            src,
+            place(r, shard, pieces[part]),
+            z_send.at[side, step, part],
+            z_recv.at[side, step, part],
+            {"dp": target},
+        )
+
+    def c_copy(shard, part, side, step):
+        spot = place(r, shard, pieces[part])
+        return remote(
+            spot, spot, c_send.at[side, step, part], c_recv.at[side, step, part], {"rows": other}
+        )
+
+    def y_copy(shard, side, step):
+        spot = place(r, shard, pieces[0])
+        return remote(
+            spot, spot, y_send.at[side, step], y_recv.at[side, step], {"tm": b_target}
+        )
+
+    def d_copy(shard, side, step):
+        spot = place(r, shard, far_piece)
+        return remote(spot, spot, d_send.at[side, step], d_recv.at[side, step], {"rows": other})
 
     def shard_of(step, side):
         return i - 1 - step if side == 0 else i + 1 + step
@@ -133,40 +176,48 @@
 
     for h in range(min(2, heads)):
         a_copy(h).start()
-    for part in range(PARTS):
+    for part in range(parts):
         for side in (0, 1):
             @pl.when(sends_on[side])
             def _():
-                z_copy(own_piece(part), i, part, side, part).start()
+                z_copy(own_piece(part), i, part, side, 0).start()
     own_spot = wbuf.at[pl.ds(pl.multiple_of((r * ndp + i) * rows, 16), rows)]
     own_copy = pltpu.make_async_copy(w_ref, own_spot, own_local)
     own_copy.start()
     own_across = remote(w_ref, own_spot, own_send, own_recv, {"rows": other})
     own_across.start()
+    for h in range(2, heads):
+        deinterleave(h)
+
     if not relay:
         @pl.when(b_sends)
         def _():
             for h in range(heads):
                 b_copy(h).start()
 
-    @pl.when(jnp.logical_not(has_b))
-    def _():
-        b_buf[...] = jnp.zeros_like(b_buf)
-
-    def weight_event(event):
-        step, part = event // PARTS, event % PARTS
+    def weight_event(step, part):
         for side in (0, 1):
             @pl.when(valid(step, side))
             def _():
                 shard = shard_of(step, side)
-                spot = place(r, shard, part)
-                z_copy(spot, shard, part, side, event).wait_recv()
+                spot = place(r, shard, pieces[part])
+                z_copy(spot, shard, part, side, step).wait_recv()
 
                 @pl.when(sends_on[side])
                 def _():
-                    z_copy(spot, shard, part, side, event + PARTS).start()
-
-                c_copy(shard, part, side, event).start()
+                    z_copy(spot, shard, part, side, step + 1).start()
+
+                if shared and part == 0:
+                    y_copy(shard, side, step).start()
+                c_copy(shard, part, side, step).start()
+
+    def far_event(step):
+        for side in (0, 1):
+            @pl.when(valid(step, side))
+            def _():
+                shard = shard_of(step, side)
+                y_copy(shard, side, step).wait_recv()
+                d_copy(shard, side, step).start()
 
     def is_live(code):
         hit = off_ref[0] == code
@@ -209,7 +260,7 @@
             )
         return (acc / total).astype(jnp.bfloat16)
 
-    done = 0
+    done = far_done = 0
     for h in range(heads + 1):
         if h < heads:
             a_copy(h).wait_recv()
@@ -220,9 +271,13 @@
                 def _():
                     b_copy(h).start()
         if ndp == 4:
-            for _ in range(PLAN.get(h, 0)):
-                weight_event(done)
+            near, far = PLAN.get(h, (0, 0))
+            for _ in range(near):
+                weight_event(done // parts, done % parts)
                 done += 1
+            for _ in range(far if shared else 0):
+                far_event(far_done)
+                far_done += 1
         if h > 0:
             g = h - 1
 
@@ -237,34 +292,64 @@
     across = remote(att_send, att.at[r], att_sem.at[0], att_sem.at[1], {"rows": other})
     across.start()
 
-    def later(event, carry):
-        weight_event(event)
-        return carry
-
-    lax.fori_loop(done, events, later, 0)
-
     own_copy.wait()
     own_across.wait_recv()
     across.wait_recv()
-
-    def settle(event, carry):
-        step, part = event // PARTS, event % PARTS
-        for side in (0, 1):
-            @pl.when(valid(step, side))
-            def _():
-                c_copy(shard_of(step, side), part, side, event).wait_recv()
-        return carry
-
-    lax.fori_loop(0, events, settle, 0)
-
-    half = wbuf.shape[0] // 2
+    for half in (0, 1):
+        for shard in range(ndp):
+            att_cut[half, shard] = att[half, :, shard * rows : (shard + 1) * rows]
     width = out_ref.shape[1]
     tile = 512 if width % 512 == 0 else width
+
+    def product(shard, columns):
+        halves = []
+        for half in (0, 1):
+            start = pl.multiple_of((half * ndp + shard) * rows, 16)
+            halves.append(
+                jnp.dot(
+                    att_cut[half, shard],
+                    wbuf[pl.ds(start, rows), columns],
+                    preferred_element_type=jnp.float32,
+                )
+            )
+        return halves[0] + halves[1]
+
     for start in range(0, width, tile):
         columns = pl.ds(start, tile)
-        product = jnp.dot(att[0], wbuf[:half, columns], preferred_element_type=jnp.float32)
-        product += jnp.dot(att[1], wbuf[half:, columns], preferred_element_type=jnp.float32)
-        out_ref[:, columns] = (gate_ref[:, columns] * product).astype(out_ref.dtype)
+        total_ref[:, columns] = product(i, columns)
+
+    def arrive(step):
+        for side in (0, 1):
+            @pl.when(valid(step, side))
+            def _():
+                shard = shard_of(step, side)
+                for part in range(parts):
+                    c_copy(shard, part, side, step).wait_recv()
+                if shared:
+                    d_copy(shard, side, step).wait_recv()
+                for start in range(0, width, tile):
+                    columns = pl.ds(start, tile)
+                    total_ref[:, columns] += product(shard, columns)
+
+    if ndp == 4:
+        for step in range(steps):
+            for event in range(max(done, step * parts), (step + 1) * parts):
+                weight_event(step, event % parts)
+            if shared and far_done <= step:
+                far_event(step)
+            arrive(step)
+    else:
+        def advance(step, carry):
+            for part in range(parts):
+                weight_event(step, part)
+            if shared:
+                far_event(step)
+            arrive(step)
+            return carry
+
+        lax.fori_loop(0, steps, advance, 0)
+
+    out_ref[...] = (gate_ref[...] * total_ref[...]).astype(out_ref.dtype)
 
     for h in range(heads):
         a_copy(h).wait_send()
@@ -277,30 +362,31 @@
     own_across.wait_send()
     across.wait_send()
 
-    def sent_own(part, carry):
+    for part in range(parts):
         for side in (0, 1):
             @pl.when(sends_on[side])
             def _():
-                z_copy(own_piece(part), i, part, side, part).wait_send()
+                z_copy(own_piece(part), i, part, side, 0).wait_send()
+
+    def sent(step, carry):
+        for side in (0, 1):
+            @pl.when(valid(step, side))
+            def _():
+                shard = shard_of(step, side)
+                for part in range(parts):
+                    c_copy(shard, part, side, step).wait_send()
+
+                    @pl.when(sends_on[side])
+                    def _():
+                        spot = place(r, shard, pieces[part])
+                        z_copy(spot, shard, part, side, step + 1).wait_send()
+
+                if shared:
+                    y_copy(shard, side, step).wait_send()
+                    d_copy(shard, side, step).wait_send()
         return carry
 
-    for part in range(PARTS):
-        sent_own(part, 0)
-
-    def sent(event, carry):
-        step, part = event // PARTS, event % PARTS
-        for side in (0, 1):
-            @pl.when(valid(step, side))
-            def _():
-                shard = shard_of(step, side)
-                c_copy(shard, part, side, event).wait_send()
-
-                @pl.when(sends_on[side])
-                def _():
-                    z_copy(place(r, shard, part), shard, part, side, event + PARTS).wait_send()
-        return carry
-
-    lax.fori_loop(0, events, sent, 0)
+    lax.fori_loop(0, steps, sent, 0)
 
 
 def local(queries, keys_values, window_offsets, out_weight, gate):
@@ -310,8 +396,7 @@
     assert queries.shape[2] == queries.shape[3] == 1 and bands == 2 and ntm % 2 == 0
     band = tl // bands
     rows, dout = out_weight.shape
-    events = PARTS * (ndp - 1)
-    kv = keys_values.reshape(tl, 2, heads, HD).transpose(2, 1, 0, 3)
+    kv = keys_values.reshape(tl, 2, width)
     bf16 = jnp.bfloat16
     vmem = pl.BlockSpec(memory_space=pltpu.VMEM)
     dma = pltpu.SemaphoreType.DMA
@@ -323,17 +408,24 @@
         scratch_shapes=[
             pltpu.VMEM((heads, 2, tl, HD), bf16),
             pltpu.VMEM((heads, 2, tl, HD), bf16),
+            pltpu.VMEM((heads, 2, tl, HD), bf16),
             pltpu.VMEM((2 * ndp * rows, dout), bf16),
             pltpu.VMEM((2, band, width), bf16),
             pltpu.VMEM((band, width), bf16),
+            pltpu.VMEM((2, ndp, band, rows), bf16),
+            pltpu.VMEM((band, dout), jnp.float32),
             dma((heads,)),
             dma((heads,)),
             dma((heads,)),
             dma((heads,)),
-            dma((2, events + PARTS)),
-            dma((2, events + PARTS)),
-            dma((2, events)),
-            dma((2, events)),
+            dma((2, ndp, 3)),
+            dma((2, ndp, 3)),
+            dma((2, ndp, 3)),
+            dma((2, ndp, 3)),
+            dma((2, ndp)),
+            dma((2, ndp)),
+            dma((2, ndp)),
+            dma((2, ndp)),
             dma,
             dma,
             dma,

time: 52.5 us -> 53.3 us (1.015)
  the two profiles are of different devices: /device:TPU:1 before, /device:TPU:11 now
where the time goes in v2:
time: 53.3 us; the launch traced here: 52.3 us
  Pallas kernels  46.7 us (88%)
  local copies, waits for them, and re-layouts  5.56 us (10%)
    pallas_call x1, Pallas kernels, local(): pl.pallas_call(functools.partial(kernel, ndp, ntm, heads), out_shape=jax....  46.7 us
    unnamed x11, local copies, waits for them, and re-layouts  5.56 us

profile of v2, /device:TPU:11, one launch (start us, length us, event | category | flops | bytes accessed | tf_op | source)
XLA Modules:
  0.0 52.3 jit_solution(8772894287915363145)
XLA Ops:
  0.0 0.0 copy-start
  0.0 1.3 %copy-done = bf16[1,1,1,1,384,2,768]{6,5,4,3,2,1,0:T(2,128)(2,1)S(1)} copy-done((bf16[1,1,1,1,384,2,768]{6,5,4,3,2,1,0:T(2,128)(2,1)S(1)}, bf16[1,1,1,1,384,2,768]{6,5,4,3,2,1,0:T(2,128)(2,1)}, u32[]{:S(2)}) %copy-start) | copy-done | bytes 1179672
  1.3 0.0 copy-start.1
  1.3 1.1 %copy-done.1 = bf16[1,1,1,1,384,768]{5,4,3,2,1,0:T(8,128)(2,1)S(1)} copy-done((bf16[1,1,1,1,384,768]{5,4,3,2,1,0:T(8,128)(2,1)S(1)}, bf16[1,1,1,1,384,768]{5,4,3,2,1,0:T(8,128)(2,1)}, u32[]{:S(2)}) %copy-start.1) | copy-done | bytes 589848
  2.3 0.0 copy-start.2
  2.3 1.1 %copy-done.2 = bf16[192,1536]{1,0:T(8,128)(2,1)S(1)} copy-done((bf16[192,1536]{1,0:T(8,128)(2,1)S(1)}, bf16[192,1536]{1,0:T(8,128)(2,1)}, u32[]{:S(2)}) %copy-start.2) | copy-done | bytes 589848
  3.4 0.0 copy-start.3
  3.4 0.7 %copy-done.3 = f32[1,1536]{1,0:T(1,128)S(1)} copy-done((f32[1,1536]{1,0:T(1,128)S(1)}, f32[1,1536]{1,0:T(1,128)}, u32[]{:S(2)}) %copy-start.3) | copy-done | bytes 6168
  4.1 0.0 copy-start.4
  4.1 0.7 %copy-done.4 = s32[1,1,1,1,3]{4,3,2,1,0:T(1,128)S(1)} copy-done((s32[1,1,1,1,3]{4,3,2,1,0:T(1,128)S(1)}, s32[1,1,1,1,3]{4,3,2,1,0:T(1,128)}, u32[]{:S(2)}) %copy-start.4) | copy-done | bytes 36
  4.7 46.7 %shard_map.55 = bf16[192,1536]{1,0:T(8,128)(2,1)S(1)} custom-call(s32[3]{0:T(128)S(1)} %bitcast.7, bf16[384,768]{1,0:T(8,128)(2,1)S(1)} %bitcast.6, bf16[384,2,768]{2,1,0:T(2,128)(2,1)S(1)} %bitcast.5, bf16[192,1536]{1,0:T(8,128)(2,1)S(1)} %copy-done.2, f32[1,1536]{1,0:T(1,128)S(1)} %copy-done.3), custom_call_target="tpu_custom_call" | custom-call | flops 2264924160 | bytes 2949120 | tf_op jit(solution)/shard_map/pallas_call | solution.py:403
  51.4 0.8 %copy.7 = bf16[1,1,1,1,192,1536]{5,4,3,2,1,0:T(8,128)(2,1)} copy(bf16[1,1,1,1,192,1536]{5,4,3,2,1,0:T(8,128)(2,1)S(1)} %bitcast.4) | data formatting | bytes 1179648
Async XLA Ops:
  0.0 1.3 %copy-start = (bf16[1,1,1,1,384,2,768]{6,5,4,3,2,1,0:T(2,128)(2,1)S(1)}, bf16[1,1,1,1,384,2,768]{6,5,4,3,2,1,0:T(2,128)(2,1)}, u32[]{:S(2)}) copy-start(bf16[1,1,1,1,384,2,768]{6,5,4,3,2,1,0:T(2,128)(2,1)} %param.6) | copy-start | bytes 3538948
  1.3 1.1 %copy-start.1 = (bf16[1,1,1,1,384,768]{5,4,3,2,1,0:T(8,128)(2,1)S(1)}, bf16[1,1,1,1,384,768]{5,4,3,2,1,0:T(8,128)(2,1)}, u32[]{:S(2)}) copy-start(bf16[1,1,1,1,384,768]{5,4,3,2,1,0:T(8,128)(2,1)} %param.5) | copy-start | bytes 1769476
  2.3 1.1 %copy-start.2 = (bf16[192,1536]{1,0:T(8,128)(2,1)S(1)}, bf16[192,1536]{1,0:T(8,128)(2,1)}, u32[]{:S(2)}) copy-start(bf16[192,1536]{1,0:T(8,128)(2,1)} %w_ref.1) | copy-start | bytes 1769476
  3.4 0.7 %copy-start.3 = (f32[1,1536]{1,0:T(1,128)S(1)}, f32[1,1536]{1,0:T(1,128)}, u32[]{:S(2)}) copy-start(f32[1,1536]{1,0:T(1,128)} %gate_ref.1) | copy-start | bytes 18436
  4.1 0.7 %copy-start.4 = (s32[1,1,1,1,3]{4,3,2,1,0:T(1,128)S(1)}, s32[1,1,1,1,3]{4,3,2,1,0:T(1,128)}, u32[]{:S(2)}) copy-start(s32[1,1,1,1,3]{4,3,2,1,0:T(1,128)} %param.7) | copy-start | bytes 40

commit v3 on v2

--- a/solution.py
+++ b/solution.py
@@ -10,25 +10,30 @@
 
 HD = 128
 MESH = pl.DeviceIdType.MESH
-PLAN = {0: (1, 0), 1: (1, 1), 2: (2, 0), 3: (1, 0), 4: (1, 1), 5: (1, 0), 6: (1, 1)}
+PLAN = {0: (1, 0), 1: (1, 0), 2: (2, 1), 3: (1, 0), 4: (1, 0), 5: (1, 1), 6: (1, 0)}
+AHEAD = 3
 
 
 def kernel(
     ndp,
     ntm,
     heads,
+    off_hbm,
+    q_hbm,
+    kv_hbm,
+    w_ref,
+    gate_hbm,
+    out_ref,
     off_ref,
     q_ref,
     kv_in,
-    w_ref,
     gate_ref,
-    out_ref,
     kv_ref,
     a_buf,
     b_buf,
     wbuf,
-    att,
-    att_send,
+    att_own,
+    att_other,
     att_cut,
     total_ref,
     a_send,
@@ -46,7 +51,9 @@
     own_send,
     own_recv,
     own_local,
-    att_sem,
+    att_send,
+    att_recv,
+    in_sem,
 ):
     i = lax.axis_index("dp")
     t = lax.axis_index("tm")
@@ -87,6 +94,15 @@
     def deinterleave(h):
         kv_ref[h] = jnp.swapaxes(kv_in[:, :, h * HD : (h + 1) * HD], 0, 1)
 
+    loads = [
+        pltpu.make_async_copy(src, dst, in_sem.at[k])
+        for k, (src, dst) in enumerate(
+            ((kv_hbm, kv_in), (q_hbm, q_ref), (gate_hbm, gate_ref), (off_hbm, off_ref))
+        )
+    ]
+    for load in loads:
+        load.start()
+
     barrier = pltpu.get_barrier_semaphore()
 
     def greet(device):
@@ -107,7 +123,8 @@
     def _():
         greet({"dp": right})
 
-    for h in range(min(2, heads)):
+    loads[0].wait()
+    for h in range(min(AHEAD, heads)):
         deinterleave(h)
 
     @pl.when(jnp.logical_not(has_b))
@@ -124,12 +141,22 @@
             src_ref=src, dst_ref=dst, send_sem=send, recv_sem=recv, device_id=device, device_id_type=MESH
         )
 
-    def a_copy(h):
-        return remote(kv_ref.at[h], a_buf.at[h], a_send.at[h], a_recv.at[h], {"tm": partner})
-
-    def b_copy(h):
+    def a_copy(h, s):
+        return remote(
+            kv_ref.at[h, s], a_buf.at[h, s], a_send.at[h, s], a_recv.at[h, s], {"tm": partner}
+        )
+
+    def b_copy(h, s):
         src = a_buf if relay else kv_ref
-        return remote(src.at[h], b_buf.at[h], b_send.at[h], b_recv.at[h], {"tm": b_target})
+        return remote(
+            src.at[h, s], b_buf.at[h, s], b_send.at[h, s], b_recv.at[h, s], {"tm": b_target}
+        )
+
+    def across(h):
+        theirs = pl.ds(pl.multiple_of(other * band, 16), band)
+        return remote(
+            att_own.at[h, theirs], att_other.at[h], att_send.at[h], att_recv.at[h], {"rows": other}
+        )
 
     def place(half, shard, spot):
         start = pl.multiple_of((half * ndp + shard) * rows + spot[0], 16)
@@ -174,8 +201,9 @@
 
     sends_on = (has_right, has_left)
 
-    for h in range(min(2, heads)):
-        a_copy(h).start()
+    for h in range(min(AHEAD, heads)):
+        for s in (0, 1):
+            a_copy(h, s).start()
     for part in range(parts):
         for side in (0, 1):
             @pl.when(sends_on[side])
@@ -186,14 +214,15 @@
     own_copy.start()
     own_across = remote(w_ref, own_spot, own_send, own_recv, {"rows": other})
     own_across.start()
-    for h in range(2, heads):
+    for h in range(AHEAD, heads):
         deinterleave(h)
 
     if not relay:
         @pl.when(b_sends)
         def _():
             for h in range(heads):
-                b_copy(h).start()
+                for s in (0, 1):
+                    b_copy(h, s).start()
 
     def weight_event(step, part):
         for side in (0, 1):
@@ -218,6 +247,9 @@
                 shard = shard_of(step, side)
                 y_copy(shard, side, step).wait_recv()
                 d_copy(shard, side, step).start()
+
+    for load in loads[1:]:
+        load.wait()
 
     def is_live(code):
         hit = off_ref[0] == code
@@ -240,36 +272,36 @@
             q, keys, (((1,), (1,)), ((), ())), preferred_element_type=jnp.float32
         )
 
-    def attend(h, which):
-        q = q_ref[pl.ds(pl.multiple_of(which * band, 16), band), h * HD : (h + 1) * HD]
-        parts = (
-            score(q, kv_ref[h, 0]),
-            score(q, a_buf[h, 0]) + a_bias,
-            score(q, b_buf[h, 0]) + b_bias,
-        )
+    def attend(h):
+        q = q_ref[:, h * HD : (h + 1) * HD]
+        held = (kv_ref, a_buf, b_buf)
+        biases = (jnp.float32(0), a_bias, b_bias)
+        scores = [score(q, buf[h, 0]) for buf in held]
         top = functools.reduce(
-            jnp.maximum, [jnp.max(s, axis=1, keepdims=True) for s in parts]
-        )
-        total = 0.0
+            jnp.maximum,
+            [jnp.max(s, axis=1, keepdims=True) + bias for s, bias in zip(scores, biases)],
+        )
+        top = top * factor
+        ones = jnp.ones((kv_in.shape[0], HD), jnp.bfloat16)
         acc = 0.0
-        for s, held in zip(parts, (kv_ref, a_buf, b_buf)):
-            p = jnp.exp2((s - top) * factor)
-            total = total + jnp.sum(p, axis=1, keepdims=True)
-            acc = acc + jnp.dot(
-                p.astype(jnp.bfloat16), held[h, 1], preferred_element_type=jnp.float32
-            )
-        return (acc / total).astype(jnp.bfloat16)
+        for s, bias, buf in zip(scores, biases, held):
+            p = jnp.exp2(s * factor - (top - bias)).astype(jnp.bfloat16)
+            values = jnp.concatenate([buf[h, 1], ones], axis=1)
+            acc = acc + jnp.dot(p, values, preferred_element_type=jnp.float32)
+        att_own[h] = (acc[:, :HD] / acc[:, HD:]).astype(jnp.bfloat16)
+        across(h).start()
 
     done = far_done = 0
-    for h in range(heads + 1):
+    for h in range(heads + 2):
         if h < heads:
-            a_copy(h).wait_recv()
-            if h + 2 < heads:
-                a_copy(h + 2).start()
-            if relay:
-                @pl.when(b_sends)
-                def _():
-                    b_copy(h).start()
+            for s in (0, 1):
+                a_copy(h, s).wait_recv()
+                if relay:
+                    @pl.when(b_sends)
+                    def _():
+                        b_copy(h, s).start()
+                if h + AHEAD < heads:
+                    a_copy(h + AHEAD, s).start()
         if ndp == 4:
             near, far = PLAN.get(h, (0, 0))
             for _ in range(near):
@@ -278,26 +310,27 @@
             for _ in range(far if shared else 0):
                 far_event(far_done)
                 far_done += 1
-        if h > 0:
-            g = h - 1
+        if h > 1:
+            g = h - 2
 
             @pl.when(has_b)
             def _():
-                b_copy(g).wait_recv()
-
-            columns = pl.ds(g * HD, HD)
-            att_send[:, columns] = attend(g, other)
-            att[r, :, columns] = attend(g, r)
-
-    across = remote(att_send, att.at[r], att_sem.at[0], att_sem.at[1], {"rows": other})
-    across.start()
+                for s in (0, 1):
+                    b_copy(g, s).wait_recv()
+
+            attend(g)
 
     own_copy.wait()
     own_across.wait_recv()
-    across.wait_recv()
-    for half in (0, 1):
-        for shard in range(ndp):
-            att_cut[half, shard] = att[half, :, shard * rows : (shard + 1) * rows]
+    for h in range(heads):
+        across(h).wait_recv()
+    mine = pl.ds(pl.multiple_of(r * band, 16), band)
+    own_half = jnp.concatenate([att_own[h, mine] for h in range(heads)], axis=1)
+    other_half = jnp.concatenate([att_other[h] for h in range(heads)], axis=1)
+    for shard in range(ndp):
+        columns = slice(shard * rows, (shard + 1) * rows)
+        att_cut[r, shard] = own_half[:, columns]
+        att_cut[other, shard] = other_half[:, columns]
     width = out_ref.shape[1]
     tile = 512 if width % 512 == 0 else width
 
@@ -352,15 +385,17 @@
     out_ref[...] = (gate_ref[...] * total_ref[...]).astype(out_ref.dtype)
 
     for h in range(heads):
-        a_copy(h).wait_send()
+        across(h).wait_send()
+        for s in (0, 1):
+            a_copy(h, s).wait_send()
 
     @pl.when(b_sends)
     def _():
         for h in range(heads):
-            b_copy(h).wait_send()
+            for s in (0, 1):
+                b_copy(h, s).wait_send()
 
     own_across.wait_send()
-    across.wait_send()
 
     for part in range(parts):
         for side in (0, 1):
@@ -399,25 +434,30 @@
     kv = keys_values.reshape(tl, 2, width)
     bf16 = jnp.bfloat16
     vmem = pl.BlockSpec(memory_space=pltpu.VMEM)
+    hbm = pl.BlockSpec(memory_space=pltpu.HBM)
     dma = pltpu.SemaphoreType.DMA
     mixed = pl.pallas_call(
         functools.partial(kernel, ndp, ntm, heads),
         out_shape=jax.ShapeDtypeStruct((band, dout), bf16),
-        in_specs=[pl.BlockSpec(memory_space=pltpu.SMEM), vmem, vmem, vmem, vmem],
+        in_specs=[hbm] * 5,
         out_specs=vmem,
         scratch_shapes=[
+            pltpu.SMEM((window_offsets.size,), jnp.int32),
+            pltpu.VMEM((tl, width), bf16),
+            pltpu.VMEM((tl, 2, width), bf16),
+            pltpu.VMEM((1, dout), jnp.float32),
             pltpu.VMEM((heads, 2, tl, HD), bf16),
             pltpu.VMEM((heads, 2, tl, HD), bf16),
             pltpu.VMEM((heads, 2, tl, HD), bf16),
             pltpu.VMEM((2 * ndp * rows, dout), bf16),
-            pltpu.VMEM((2, band, width), bf16),
-            pltpu.VMEM((band, width), bf16),
+            pltpu.VMEM((heads, tl, HD), bf16),
+            pltpu.VMEM((heads, band, HD), bf16),
             pltpu.VMEM((2, ndp, band, rows), bf16),
             pltpu.VMEM((band, dout), jnp.float32),
-            dma((heads,)),
-            dma((heads,)),
-            dma((heads,)),
-            dma((heads,)),
+            dma((heads, 2)),
+            dma((heads, 2)),
+            dma((heads, 2)),
+            dma((heads, 2)),
             dma((2, ndp, 3)),
             dma((2, ndp, 3)),
             dma((2, ndp, 3)),
@@ -429,10 +469,12 @@
             dma,
             dma,
             dma,
-            dma((2,)),
+            dma((heads,)),
+            dma((heads,)),
+            dma((4,)),
         ],
         compiler_params=pltpu.CompilerParams(
-            collective_id=0, has_side_effects=True, vmem_limit_bytes=48 * 1024 * 1024
+            collective_id=0, has_side_effects=True, vmem_limit_bytes=64 * 1024 * 1024
         ),
         cost_estimate=pl.CostEstimate(
             flops=4 * 3 * tl * tl * width + 4 * band * width * dout,

time: 53.3 us -> 49.6 us (0.931); the launches traced: 52.3 us -> 49.4 us
  local copies, waits for them, and re-layouts: 5.56 us -> 1.92 us
  Pallas kernels: 46.7 us -> 47.5 us
    unnamed x11 -> x1, local copies, waits for them, and re-layouts: 5.56 us -> 1.92 us
    pallas_call x1, Pallas kernels: 46.7 us -> 47.5 us  [local(): pl.pallas_call(functools.partial(kernel, ndp, ntm, heads), out_shape=jax....]
where the time goes in v3:
time: 49.6 us; the launch traced here: 49.4 us
  Pallas kernels  47.5 us (96%)
  local copies, waits for them, and re-layouts  1.92 us (4%)
    pallas_call x1, Pallas kernels, local(): pl.pallas_call(functools.partial(kernel, ndp, ntm, heads), out_shape=jax....  47.5 us
    unnamed x1, local copies, waits for them, and re-layouts  1.92 us

profile of v3, /device:TPU:11, one launch (start us, length us, event | category | flops | bytes accessed | tf_op | source)
XLA Modules:
  0.0 49.4 jit_solution(4910497798091225543)
XLA Ops:
  0.0 47.5 %shard_map.55 = bf16[192,1536]{1,0:T(8,128)(2,1)} custom-call(s32[3]{0:T(128)} %bitcast.7, bf16[384,768]{1,0:T(8,128)(2,1)} %bitcast.6, bf16[384,2,768]{2,1,0:T(2,128)(2,1)} %bitcast.5, bf16[192,1536]{1,0:T(8,128)(2,1)} %w_ref.1, f32[1,1536]{1,0:T(1,128)} %gate_hbm.1), custom_call_target="tpu_custom_call" | custom-call | flops 2264924160 | bytes 2949120 | tf_op jit(solution)/shard_map/pallas_call | solution.py:439
  47.5 1.9 %copy.7 = bf16[1,1,1,1,192,1536]{5,4,3,2,1,0:T(8,128)(2,1)} copy(bf16[1,1,1,1,192,1536]{5,4,3,2,1,0:T(8,128)(2,1)} %bitcast.4) | data formatting | bytes 1179648

commit v4 on v3

--- a/solution.py
+++ b/solution.py
@@ -10,7 +10,7 @@
 
 HD = 128
 MESH = pl.DeviceIdType.MESH
-PLAN = {0: (1, 0), 1: (1, 0), 2: (2, 1), 3: (1, 0), 4: (1, 0), 5: (1, 1), 6: (1, 0)}
+PLAN = {0: 1, 1: 1, 2: 2, 3: 1, 4: 1, 5: 1, 6: 1}
 AHEAD = 3
 
 
@@ -34,7 +34,6 @@
     wbuf,
     att_own,
     att_other,
-    att_cut,
     total_ref,
     a_send,
     a_recv,
@@ -80,7 +79,7 @@
     rows = w_ref.shape[0]
     steps = ndp - 1
     upper = t // 2
-    if relay and rows % 192 == 0:
+    if relay and ndp == 4 and heads == 6 and rows == 192:
         edge, inner = rows // 6, rows // 3
         pieces = ((upper * (rows - edge), edge), (edge, inner), (edge + inner, inner))
         far_piece = ((1 - upper) * (rows - edge), edge)
@@ -91,8 +90,16 @@
         shared = False
     parts = len(pieces)
 
-    def deinterleave(h):
-        kv_ref[h] = jnp.swapaxes(kv_in[:, :, h * HD : (h + 1) * HD], 0, 1)
+    descending = jnp.where(i >= ndp // 2, 1, 0)
+
+    def head(g):
+        return g + descending * (heads - 1 - 2 * g)
+
+    def lanes(g):
+        return pl.ds(pl.multiple_of(head(g) * HD, HD), HD)
+
+    def deinterleave(g):
+        kv_ref[head(g)] = jnp.swapaxes(kv_in[:, :, lanes(g)], 0, 1)
 
     loads = [
         pltpu.make_async_copy(src, dst, in_sem.at[k])
@@ -141,21 +148,24 @@
             src_ref=src, dst_ref=dst, send_sem=send, recv_sem=recv, device_id=device, device_id_type=MESH
         )
 
-    def a_copy(h, s):
+    def a_copy(g, s):
+        h = head(g)
         return remote(
-            kv_ref.at[h, s], a_buf.at[h, s], a_send.at[h, s], a_recv.at[h, s], {"tm": partner}
-        )
-
-    def b_copy(h, s):
+            kv_ref.at[h, s], a_buf.at[h, s], a_send.at[g, s], a_recv.at[g, s], {"tm": partner}
+        )
+
+    def b_copy(g, s):
+        h = head(g)
         src = a_buf if relay else kv_ref
         return remote(
-            src.at[h, s], b_buf.at[h, s], b_send.at[h, s], b_recv.at[h, s], {"tm": b_target}
-        )
-
-    def across(h):
+            src.at[h, s], b_buf.at[h, s], b_send.at[g, s], b_recv.at[g, s], {"tm": b_target}
+        )
+
+    def across(g):
+        h = head(g)
         theirs = pl.ds(pl.multiple_of(other * band, 16), band)
         return remote(
-            att_own.at[h, theirs], att_other.at[h], att_send.at[h], att_recv.at[h], {"rows": other}
+            att_own.at[h, theirs], att_other.at[h], att_send.at[g], att_recv.at[g], {"rows": other}
         )
 
     def place(half, shard, spot):
@@ -236,9 +246,15 @@
                 def _():
                     z_copy(spot, shard, part, side, step + 1).start()
 
-                if shared and part == 0:
+                if shared and part == 0 and step == 0:
                     y_copy(shard, side, step).start()
                 c_copy(shard, part, side, step).start()
+
+    def relay_edge(step):
+        for side in (0, 1):
+            @pl.when(valid(step, side))
+            def _():
+                y_copy(shard_of(step, side), side, step).start()
 
     def far_event(step):
         for side in (0, 1):
@@ -272,8 +288,9 @@
             q, keys, (((1,), (1,)), ((), ())), preferred_element_type=jnp.float32
         )
 
-    def attend(h):
-        q = q_ref[:, h * HD : (h + 1) * HD]
+    def attend(g):
+        h = head(g)
+        q = q_ref[:, lanes(g)]
         held = (kv_ref, a_buf, b_buf)
         biases = (jnp.float32(0), a_bias, b_bias)
         scores = [score(q, buf[h, 0]) for buf in held]
@@ -289,10 +306,47 @@
             values = jnp.concatenate([buf[h, 1], ones], axis=1)
             acc = acc + jnp.dot(p, values, preferred_element_type=jnp.float32)
         att_own[h] = (acc[:, :HD] / acc[:, HD:]).astype(jnp.bfloat16)
-        across(h).start()
-
-    done = far_done = 0
-    for h in range(heads + 2):
+        across(g).start()
+
+    width = out_ref.shape[1]
+    tile = 512 if width % 512 == 0 else width
+    mine = pl.ds(pl.multiple_of(r * band, 16), band)
+
+    def project(p):
+        first = p + descending * (heads // 2 - 1 - 2 * p)
+        for g in (2 * p, 2 * p + 1):
+            across(g).wait_recv()
+        own = jnp.concatenate([att_own[2 * first + k, mine] for k in (0, 1)], axis=1)
+        their = jnp.concatenate([att_other[2 * first + k] for k in (0, 1)], axis=1)
+        for start in range(0, width, tile):
+            columns = pl.ds(start, tile)
+            value = 0.0
+            for half, part in ((r, own), (other, their)):
+                begin = pl.multiple_of(half * ndp * rows + first * 2 * HD, 2 * HD)
+                value += jnp.dot(
+                    part, wbuf[pl.ds(begin, 2 * HD), columns], preferred_element_type=jnp.float32
+                )
+            if p == 0:
+                total_ref[:, columns] = value
+            elif p < heads // 2 - 1:
+                total_ref[:, columns] += value
+            else:
+                value = gate_ref[:, columns] * (total_ref[:, columns] + value)
+                out_ref[:, columns] = value.astype(out_ref.dtype)
+
+    def arrive(step):
+        for side in (0, 1):
+            @pl.when(valid(step, side))
+            def _():
+                shard = shard_of(step, side)
+                for part in range(parts):
+                    c_copy(shard, part, side, step).wait_recv()
+                if shared:
+                    d_copy(shard, side, step).wait_recv()
+
+    staged = shared
+    done = 0
+    for h in range(heads + 1):
         if h < heads:
             for s in (0, 1):
                 a_copy(h, s).wait_recv()
@@ -302,16 +356,17 @@
                         b_copy(h, s).start()
                 if h + AHEAD < heads:
                     a_copy(h + AHEAD, s).start()
-        if ndp == 4:
-            near, far = PLAN.get(h, (0, 0))
-            for _ in range(near):
+        if staged:
+            for _ in range(PLAN.get(h, 0)):
                 weight_event(done // parts, done % parts)
                 done += 1
-            for _ in range(far if shared else 0):
-                far_event(far_done)
-                far_done += 1
-        if h > 1:
-            g = h - 2
+            if h == 2:
+                far_event(0)
+            if h == 5:
+                relay_edge(1)
+                relay_edge(2)
+        if h > 0:
+            g = h - 1
 
             @pl.when(has_b)
             def _():
@@ -319,70 +374,32 @@
                     b_copy(g, s).wait_recv()
 
             attend(g)
-
-    own_copy.wait()
-    own_across.wait_recv()
-    for h in range(heads):
-        across(h).wait_recv()
-    mine = pl.ds(pl.multiple_of(r * band, 16), band)
-    own_half = jnp.concatenate([att_own[h, mine] for h in range(heads)], axis=1)
-    other_half = jnp.concatenate([att_other[h] for h in range(heads)], axis=1)
-    for shard in range(ndp):
-        columns = slice(shard * rows, (shard + 1) * rows)
-        att_cut[r, shard] = own_half[:, columns]
-        att_cut[other, shard] = other_half[:, columns]
-    width = out_ref.shape[1]
-    tile = 512 if width % 512 == 0 else width
-
-    def product(shard, columns):
-        halves = []
-        for half in (0, 1):
-            start = pl.multiple_of((half * ndp + shard) * rows, 16)
-            halves.append(
-                jnp.dot(
-                    att_cut[half, shard],
-                    wbuf[pl.ds(start, rows), columns],
-                    preferred_element_type=jnp.float32,
-                )
-            )
-        return halves[0] + halves[1]
-
-    for start in range(0, width, tile):
-        columns = pl.ds(start, tile)
-        total_ref[:, columns] = product(i, columns)
-
-    def arrive(step):
-        for side in (0, 1):
-            @pl.when(valid(step, side))
-            def _():
-                shard = shard_of(step, side)
-                for part in range(parts):
-                    c_copy(shard, part, side, step).wait_recv()
-                if shared:
-                    d_copy(shard, side, step).wait_recv()
-                for start in range(0, width, tile):
-                    columns = pl.ds(start, tile)
-                    total_ref[:, columns] += product(shard, columns)
-
-    if ndp == 4:
-        for step in range(steps):
-            for event in range(max(done, step * parts), (step + 1) * parts):
-                weight_event(step, event % parts)
-            if shared and far_done <= step:
-                far_event(step)
-            arrive(step)
+            if staged and g == 3:
+                own_copy.wait()
+                own_across.wait_recv()
+                arrive(0)
+                project(0)
+
+    if staged:
+        far_event(1)
+        weight_event(2, 2)
+        arrive(1)
+        project(1)
+        far_event(2)
+        arrive(2)
+        project(2)
     else:
         def advance(step, carry):
             for part in range(parts):
                 weight_event(step, part)
-            if shared:
-                far_event(step)
-            arrive(step)
             return carry
 
         lax.fori_loop(0, steps, advance, 0)
-
-    out_ref[...] = (gate_ref[...] * total_ref[...]).astype(out_ref.dtype)
+        own_copy.wait()
+        own_across.wait_recv()
+        lax.fori_loop(0, steps, lambda step, carry: (arrive(step), carry)[1], 0)
+        for p in range(heads // 2):
+            project(p)
 
     for h in range(heads):
         across(h).wait_send()
@@ -428,7 +445,7 @@
     tl, width = queries.shape[4], queries.shape[5]
     heads = width // HD
     ndp, ntm, bands = lax.axis_size("dp"), lax.axis_size("tm"), lax.axis_size("rows")
-    assert queries.shape[2] == queries.shape[3] == 1 and bands == 2 and ntm % 2 == 0
+    assert queries.shape[2] == queries.shape[3] == 1 and bands == 2 and ntm % 2 == 0 and heads % 2 == 0
     band = tl // bands
     rows, dout = out_weight.shape
     kv = keys_values.reshape(tl, 2, width)
@@ -452,7 +469,6 @@
             pltpu.VMEM((2 * ndp * rows, dout), bf16),
             pltpu.VMEM((heads, tl, HD), bf16),
             pltpu.VMEM((heads, band, HD), bf16),
-            pltpu.VMEM((2, ndp, band, rows), bf16),
             pltpu.VMEM((band, dout), jnp.float32),
             dma((heads, 2)),
             dma((heads, 2)),

time: 49.6 us -> 47.7 us (0.962)
  Pallas kernels: 47.5 us -> 45.6 us
    pallas_call x1, Pallas kernels: 47.5 us -> 45.6 us  [local(): pl.pallas_call(functools.partial(kernel, ndp, ntm, heads), out_shape=jax....]
where the time goes in v4:
time: 47.7 us; the launch traced here: 47.6 us
  Pallas kernels  45.6 us (96%)
  local copies, waits for them, and re-layouts  1.92 us (4%)
    pallas_call x1, Pallas kernels, local(): pl.pallas_call(functools.partial(kernel, ndp, ntm, heads), out_shape=jax....  45.6 us
    unnamed x1, local copies, waits for them, and re-layouts  1.92 us

profile of v4, /device:TPU:11, one launch (start us, length us, event | category | flops | bytes accessed | tf_op | source)
XLA Modules:
  0.0 47.6 jit_solution(17867455553497170575)
XLA Ops:
  0.0 45.6 %shard_map.55 = bf16[192,1536]{1,0:T(8,128)(2,1)} custom-call(s32[3]{0:T(128)} %bitcast.7, bf16[384,768]{1,0:T(8,128)(2,1)} %bitcast.6, bf16[384,2,768]{2,1,0:T(2,128)(2,1)} %bitcast.5, bf16[192,1536]{1,0:T(8,128)(2,1)} %w_ref.1, f32[1,1536]{1,0:T(1,128)} %gate_hbm.1), custom_call_target="tpu_custom_call" | custom-call | flops 2264924160 | bytes 2949120 | tf_op jit(solution)/shard_map/pallas_call | solution.py:456
  45.6 1.9 %copy.7 = bf16[1,1,1,1,192,1536]{5,4,3,2,1,0:T(8,128)(2,1)} copy(bf16[1,1,1,1,192,1536]{5,4,3,2,1,0:T(8,128)(2,1)} %bitcast.4) | data formatting | bytes 1179648

commit v5 on v4

--- a/solution.py
+++ b/solution.py
@@ -130,14 +130,6 @@
     def _():
         greet({"dp": right})
 
-    loads[0].wait()
-    for h in range(min(AHEAD, heads)):
-        deinterleave(h)
-
-    @pl.when(jnp.logical_not(has_b))
-    def _():
-        b_buf[...] = jnp.zeros_like(b_buf)
-
     peers = 2
     for present in (greets_b, has_left, has_right):
         peers = peers + jnp.where(present, 1, 0)
@@ -211,9 +203,6 @@
 
     sends_on = (has_right, has_left)
 
-    for h in range(min(AHEAD, heads)):
-        for s in (0, 1):
-            a_copy(h, s).start()
     for part in range(parts):
         for side in (0, 1):
             @pl.when(sends_on[side])
@@ -224,6 +213,16 @@
     own_copy.start()
     own_across = remote(w_ref, own_spot, own_send, own_recv, {"rows": other})
     own_across.start()
+    loads[0].wait()
+    for h in range(min(AHEAD, heads)):
+        deinterleave(h)
+        for s in (0, 1):
+            a_copy(h, s).start()
+
+    @pl.when(jnp.logical_not(has_b))
+    def _():
+        b_buf[...] = jnp.zeros_like(b_buf)
+
     for h in range(AHEAD, heads):
         deinterleave(h)
 

time: 47.7 us -> 47 us (0.985)
  Pallas kernels: 45.6 us -> 44.9 us
    pallas_call x1, Pallas kernels: 45.6 us -> 44.9 us  [local(): pl.pallas_call(functools.partial(kernel, ndp, ntm, heads), out_shape=jax....]
where the time goes in v5:
time: 47 us; the launch traced here: 46.9 us
  Pallas kernels  44.9 us (96%)
  local copies, waits for them, and re-layouts  1.92 us (4%)
    pallas_call x1, Pallas kernels, local(): pl.pallas_call(functools.partial(kernel, ndp, ntm, heads), out_shape=jax....  44.9 us
    unnamed x1, local copies, waits for them, and re-layouts  1.92 us

profile of v5, /device:TPU:11, one launch (start us, length us, event | category | flops | bytes accessed | tf_op | source)
XLA Modules:
  0.0 46.9 jit_solution(1775467158462924809)
XLA Ops:
  0.0 44.9 %shard_map.55 = bf16[192,1536]{1,0:T(8,128)(2,1)} custom-call(s32[3]{0:T(128)} %bitcast.7, bf16[384,768]{1,0:T(8,128)(2,1)} %bitcast.6, bf16[384,2,768]{2,1,0:T(2,128)(2,1)} %bitcast.5, bf16[192,1536]{1,0:T(8,128)(2,1)} %w_ref.1, f32[1,1536]{1,0:T(1,128)} %gate_hbm.1), custom_call_target="tpu_custom_call" | custom-call | flops 2264924160 | bytes 2949120 | tf_op jit(solution)/shard_map/pallas_call | solution.py:455
  44.9 1.9 %copy.7 = bf16[1,1,1,1,192,1536]{5,4,3,2,1,0:T(8,128)(2,1)} copy(bf16[1,1,1,1,192,1536]{5,4,3,2,1,0:T(8,128)(2,1)} %bitcast.4) | data formatting | bytes 1179648
